TPU v7x, 32 devices: a whole 2x2x4 slice. The times are simulated.
32 devices in a mesh: vx: 8 (over z, x), vy: 4 (over y, core).
Axes of the slice: x: 2, y: 2, z: 4, core: 2. Of those that a mesh axis runs over, the one named last changes fastest.
Arguments:
- fields: bfloat16 [4, 512, 640, 128], P(None, 'vx', 'vy'), may hold values from -6 to 6
- modulus: bfloat16 [512, 640, 128], P('vx', 'vy'), as said below
- anchors: int32 [8, 4, 14, 3], P('vx', 'vy'), may hold values from 0 to 10, as said below
- home_count: int32 [8, 4], P('vx', 'vy'), may hold values from 1 to 14, as said below
Outputs:
- gradient: float32 [512, 640, 128], P('vx', 'vy')
Inputs may be any that keep to these rules, and one draw needn't show every extreme that they name: `anchors`: column 0 is at most 4, column 1 at most 10, column 2 at most 2. `home_count`: the counts of the 8 tiles that share a vy index sum to 56. The modulus's real parts are positive and at least three times its imaginary parts, which are positive.
All inputs are finite; a program needn't handle non-finite values.
Results may differ from a plain program's by a relative error of at most 0.0003.
Values may be sent and summed in bfloat16 or wider, within the bound.
A program may use at most 192 MiB of HBM per device.

v0:
```python
import functools

import jax
import jax.numpy as jnp
import numpy as np
from jax import lax
from jax.experimental import pallas as pl
from jax.experimental.pallas import tpu as pltpu
from jax.sharding import PartitionSpec as P

NF = 4
SUB = 32
HALO = 16
OMEGA = 0.07
LANES = 128
NZ = 64
PLANES = 8
A_PLANES = 8
FIRST = 8


def constants():
    starts = (NZ - SUB) // HALO + 1
    second = 6.0 * np.eye(SUB) - np.eye(SUB, k=1) - np.eye(SUB, k=-1)
    tri = np.kron(np.eye(NF), second)
    pick = np.zeros((starts, NF, LANES, 4, LANES))
    spread = np.zeros((starts, LANES, 2, LANES))
    gather = np.zeros((starts, 2, 2, LANES, LANES))
    for s in range(starts):
        for f in range(NF):
            for z in range(SUB):
                for part in range(2):
                    source = part * NZ + s * HALO + z
                    lane = f * SUB + z
                    pick[s, f, source, part, lane] = 1.0
                    pick[s, f, source, 2 + part] = tri[lane]
                    spread[s, source, part, lane] = 1.0
                    gather[s, part, :, lane, source] = 1.0
    bf16 = jnp.bfloat16
    return (
        jnp.asarray(pick.reshape(starts, NF * LANES, 4 * LANES), bf16),
        jnp.asarray(spread.reshape(starts, LANES, 2 * LANES), bf16),
        jnp.asarray(gather.reshape(starts, 4 * LANES, LANES), bf16),
        jnp.asarray(np.concatenate([tri, tri], axis=0), bf16),
    )


def split(value):
    high = value.astype(jnp.bfloat16)
    low = (value - high.astype(jnp.float32)).astype(jnp.bfloat16)
    return high, low


def neighbours(ref, x):
    low = ref[x, FIRST : FIRST + SUB]
    high = ref[x + 2, FIRST : FIRST + SUB]
    left = ref[x + 1, FIRST - 1 : FIRST - 1 + SUB]
    right = ref[x + 1, FIRST + 1 : FIRST + 1 + SUB]
    return (low + high) + (left + right)


def center(ref, x):
    return ref[x + 1, FIRST : FIRST + SUB]


def stencil_z(real, imag, x, tri):
    rows = PLANES * SUB
    parts = []
    for ref in (real, imag):
        value = ref[pl.ds(x + 1, PLANES), FIRST : FIRST + SUB].reshape(rows, LANES)
        parts.append(jnp.concatenate(split(value), axis=1))
    return jnp.dot(
        jnp.concatenate(parts, axis=0), tri, preferred_element_type=jnp.float32
    )


def work(group, slots, kinds, tx, ty, n_sources, *refs):
    refs = list(refs)
    take = lambda count: [refs.pop(0) for _ in range(count)]
    (info,) = take(1)
    sources = [take(2)] + [take(1) for _ in range(n_sources - 1)]
    earlier = take(group)
    pick, spread, gather, tri = take(4)
    outs = take({0: 1, 1: 1, 2: 2}[group])
    (order, buf, total, ur, ui, wr, wi, qr, qi) = take(9)
    (zur, zui, l1r, l1i, v3r, v3i, gr, gi, mur, mui) = take(10)
    sems, out_sem = take(2)
    (strip,) = take(1) if group == 2 else (None,)

    x_base = tx - HALO if group == 1 else -HALO
    blocks = (tx // HALO, ty // HALO)

    if group == 2:
        fills = [
            pltpu.make_async_copy(
                earlier[0], total.at[HALO : HALO + tx, HALO : HALO + ty], out_sem.at[0]
            ),
            pltpu.make_async_copy(earlier[1].at[:HALO], strip, out_sem.at[3]),
        ]
        for fill in fills:
            fill.start()
    for ref in (ur, ui, wr, wi, qr, qi):
        plane = jnp.zeros((FIRST + SUB + 8, LANES), jnp.float32)
        ref[0] = plane
        ref[SUB + 1] = plane

        def edge(x, carry, ref=ref):
            row = jnp.zeros((8, LANES), jnp.float32)
            ref[x, 0:FIRST] = row
            ref[x, FIRST + SUB :] = row
            return carry

        lax.fori_loop(1, SUB + 1, edge, 0)

    def clear(x, carry):
        if group == 2:
            side = jnp.zeros((HALO, LANES), jnp.float32)
            total[x, :HALO] = side
            total[x, HALO + ty :] = side
        else:
            total[x] = jnp.zeros(total.shape[1:], jnp.float32)
        return carry

    lax.fori_loop(0, total.shape[0], clear, 0)
    if group == 2:
        total[:HALO, HALO : HALO + ty] = jnp.zeros((HALO, ty, LANES), jnp.float32)

    def listed(slot, count):
        mine = info[4 * slot] == kinds

        @pl.when(mine)
        def _():
            order[count] = slot

        return count + jnp.where(mine, 1, 0)

    count = lax.fori_loop(0, slots, listed, jnp.int32(0))

    def place(item):
        slot = order[item]
        return info[4 * slot + 1], info[4 * slot + 2], info[4 * slot + 3]

    def transfers(item, slot, starting):
        bx0, by0, _ = place(item)
        for dx in range(2):
            for dy in range(2):
                bx, by = bx0 + dx, by0 + dy
                rows = pl.ds(dx * HALO, HALO)
                cols = pl.ds(dy * HALO, HALO)
                to_f = buf.at[slot, :NF, rows, cols, :]
                to_m = buf.at[slot, NF, rows, cols, :]
                to_all = buf.at[slot, :, rows, cols, :]
                quarter = 2 * dx + dy
                outside = (bx < 0) | (by < 0)
                past_x = bx >= blocks[0]
                past_y = by >= blocks[1]
                conditions = [jnp.logical_not(past_x) & jnp.logical_not(past_y)]
                if n_sources > 1:
                    conditions.append(jnp.logical_not(past_x) & past_y)
                if n_sources > 2:
                    conditions.append(past_x & jnp.logical_not(past_y))
                    conditions.append(past_x & past_y)
                for kind, condition in enumerate(conditions):
                    @pl.when(jnp.logical_not(outside) & condition)
                    def _(kind=kind):
                        r = 0 if kind >= 2 else pl.multiple_of(bx * HALO, HALO)
                        c = 0 if kind in (1, 3) else pl.multiple_of(by * HALO, HALO)
                        box = (pl.ds(r, HALO), pl.ds(c, HALO), slice(None))
                        first = sources[kind][0].at[(slice(None),) + box]
                        if kind == 0:
                            pairs = [(first, to_f), (sources[0][1].at[box], to_m)]
                        else:
                            pairs = [(first, to_all)]
                        for which, (a, b) in enumerate(pairs):
                            copy = pltpu.make_async_copy(a, b, sems.at[slot, quarter, which])
                            if starting:
                                copy.start()
                            else:
                                copy.wait()
                if starting:
                    @pl.when(outside)
                    def _():
                        buf[slot, :, dx * HALO : dx * HALO + HALO, dy * HALO : dy * HALO + HALO, :] = jnp.zeros(
                            (NF + 1, HALO, HALO, LANES), jnp.bfloat16
                        )

    @pl.when(count > 0)
    def _():
        transfers(jnp.int32(0), 0, True)

    def subzone(item, carry):
        slot = lax.rem(item, 2)

        @pl.when(item + 1 < count)
        def _():
            transfers(item + 1, 1 - slot, True)

        transfers(item, slot, False)
        bx0, by0, depth = place(item)

        def load(step, carry):
            x = step * A_PLANES
            rows = A_PLANES * SUB
            shape = (A_PLANES, SUB, LANES)
            block = jnp.concatenate(
                [buf[slot, f, pl.ds(x, A_PLANES)].reshape(rows, LANES) for f in range(NF)], axis=1
            )
            got = jnp.dot(block, pick[depth], preferred_element_type=jnp.float32)
            ur[pl.ds(x + 1, A_PLANES), FIRST : FIRST + SUB] = got[:, :LANES].reshape(shape)
            ui[pl.ds(x + 1, A_PLANES), FIRST : FIRST + SUB] = got[:, LANES : 2 * LANES].reshape(shape)
            zur[pl.ds(x, A_PLANES)] = got[:, 2 * LANES : 3 * LANES].reshape(shape)
            zui[pl.ds(x, A_PLANES)] = got[:, 3 * LANES :].reshape(shape)
            stiff = buf[slot, NF, pl.ds(x, A_PLANES)].reshape(rows, LANES)
            mu = jnp.dot(stiff, spread[depth], preferred_element_type=jnp.float32)
            mur[pl.ds(x, A_PLANES)] = mu[:, :LANES].reshape(shape)
            mui[pl.ds(x, A_PLANES)] = mu[:, LANES:].reshape(shape)
            return carry

        lax.fori_loop(0, SUB // A_PLANES, load, 0)

        def second(step, carry):
            for p in range(PLANES):
                x = step * PLANES + p
                ir = OMEGA * (zur[x] - neighbours(ur, x))
                ii = OMEGA * (zui[x] - neighbours(ui, x))
                l1r[x] = ir
                l1i[x] = ii
                mr, mi = mur[x], mui[x]
                keep = OMEGA * (2.0 - OMEGA)
                wr[x + 1, FIRST : FIRST + SUB] = keep * center(ur, x) - OMEGA * (mr * ir - mi * ii)
                wi[x + 1, FIRST : FIRST + SUB] = keep * center(ui, x) - OMEGA * (mr * ii + mi * ir)
            return carry

        lax.fori_loop(0, SUB // PLANES, second, 0)

        def third(step, carry):
            z = stencil_z(wr, wi, step * PLANES, tri[...])
            for p in range(PLANES):
                x = step * PLANES + p
                ir = z[p * SUB : (p + 1) * SUB] - neighbours(wr, x)
                ii = z[(PLANES + p) * SUB : (PLANES + p + 1) * SUB] - neighbours(wi, x)
                mr, mi = mur[x], mui[x]
                vr = (1.0 - OMEGA) * (center(wr, x) - center(ur, x)) - OMEGA * (mr * ir - mi * ii)
                vi = (1.0 - OMEGA) * (center(wi, x) - center(ui, x)) - OMEGA * (mr * ii + mi * ir)
                v3r[x] = vr
                v3i[x] = vi
                qr[x + 1, FIRST : FIRST + SUB] = mr * vr + mi * vi
                qi[x + 1, FIRST : FIRST + SUB] = mr * vi - mi * vr
                gr[x] = vr * ir + vi * ii
                gi[x] = vi * ir - vr * ii
            return carry

        lax.fori_loop(0, SUB // PLANES, third, 0)

        row0 = bx0 * HALO - x_base
        col0 = pl.multiple_of((by0 + 1) * HALO, HALO)

        def fourth(step, carry):
            z = stencil_z(qr, qi, step * PLANES, tri[...])
            parts = []
            for p in range(PLANES):
                x = step * PLANES + p
                jr = z[p * SUB : (p + 1) * SUB] - neighbours(qr, x)
                ji = z[(PLANES + p) * SUB : (PLANES + p + 1) * SUB] - neighbours(qi, x)
                vr = (1.0 - OMEGA) * v3r[x] - OMEGA * jr
                vi = (1.0 - OMEGA) * v3i[x] - OMEGA * ji
                ir, ii = l1r[x], l1i[x]
                sr = -OMEGA * (gr[x] + (vr * ir + vi * ii))
                si = -OMEGA * (gi[x] + (vi * ir - vr * ii))
                parts.append(jnp.concatenate(split(sr) + split(si), axis=1))
            grad = jnp.dot(
                jnp.concatenate(parts, axis=0), gather[depth], preferred_element_type=jnp.float32
            )
            for p in range(PLANES):
                x = step * PLANES + p
                total[row0 + x, pl.ds(col0, SUB)] += grad[p * SUB : (p + 1) * SUB]
            return carry

        lax.fori_loop(0, SUB // PLANES, fourth, 0)
        return carry

    if group == 2:
        for fill in fills:
            fill.wait()

        def joined(x, carry):
            total[tx + x, HALO:] += strip[x]
            return carry

        lax.fori_loop(0, HALO, joined, 0)

    lax.fori_loop(0, count, subzone, 0)

    if group == 1:
        copies = [(total.at[:, HALO : 2 * HALO + ty], outs[0])]
    else:
        copies = [(total.at[HALO : HALO + tx, HALO : HALO + ty], outs[0])]
        if group == 2:
            copies.append((total.at[HALO : HALO + tx, HALO + ty : 2 * HALO + ty], outs[1]))
    started = []
    for index, (a, b) in enumerate(copies):
        started.append(pltpu.make_async_copy(a, b, out_sem.at[1 + index]))
        started[-1].start()
    for copy in started:
        copy.wait()


def run(group, info, sources, mats, tx, ty, *earlier):
    slots = info.shape[0] // 4
    f32 = jnp.float32
    total_rows = 2 * HALO if group == 1 else HALO + tx
    outs = {
        0: [(tx, ty, LANES)],
        1: [(2 * HALO, HALO + ty, LANES)],
        2: [(tx, ty, LANES), (tx, HALO, LANES)],
    }[group]
    hbm = pl.BlockSpec(memory_space=pl.ANY)
    smem = pl.BlockSpec(memory_space=pltpu.SMEM)
    vmem = pl.BlockSpec(memory_space=pltpu.VMEM)
    flat = [part for pair in sources for part in pair]
    args = [info] + flat + list(earlier) + list(mats)
    in_specs = [smem] + [hbm] * (len(args) - 1 - len(mats)) + [vmem] * len(mats)
    padded = pltpu.VMEM((SUB + 2, FIRST + SUB + 8, LANES), f32)
    plain = pltpu.VMEM((SUB, SUB, LANES), f32)
    return pl.pallas_call(
        functools.partial(work, group, slots, group, tx, ty, len(sources)),
        out_shape=[jax.ShapeDtypeStruct(shape, f32) for shape in outs],
        in_specs=in_specs,
        out_specs=[hbm] * len(outs),
        scratch_shapes=[
            pltpu.SMEM((slots,), jnp.int32),
            pltpu.VMEM((2, NF + 1, SUB, SUB, LANES), jnp.bfloat16),
            pltpu.VMEM((total_rows, 2 * HALO + ty, LANES), f32),
        ]
        + [padded] * 6
        + [plain] * 10
        + [pltpu.SemaphoreType.DMA((2, 4, 2)), pltpu.SemaphoreType.DMA((4,))]
        + ([pltpu.VMEM((HALO, HALO + ty, LANES), f32)] if group == 2 else []),
        compiler_params=pltpu.CompilerParams(vmem_limit_bytes=48 * 2**20),
        cost_estimate=pl.CostEstimate(
            flops=2 * 10**10 if group == 0 else 10**10, bytes_accessed=150 * 10**6, transcendentals=0
        ),
        name=("interior", "beyond_x", "beyond_y")[group],
    )(*args)


def shards(fields, modulus, anchors, home_count):
    tx, ty = modulus.shape[0], modulus.shape[1]
    n_x, n_y = lax.axis_size("vx"), lax.axis_size("vy")
    i, j = lax.axis_index("vx"), lax.axis_index("vy")
    both = ("vx", "vy")
    down_x = [(k + 1, k) for k in range(n_x - 1)]
    down_y = [(k + 1, k) for k in range(n_y - 1)]
    down_d = [
        ((a + 1) * n_y + b + 1, a * n_y + b) for a in range(n_x - 1) for b in range(n_y - 1)
    ]
    up_x = [(b, a) for a, b in down_x]
    up_y = [(b, a) for a, b in down_y]

    spots = anchors[0, 0]
    home = spots.shape[0]
    live = (jnp.arange(home, dtype=jnp.int32) < home_count[0, 0]).astype(jnp.int32)
    own = jnp.concatenate([spots, live[:, None]], axis=1)
    own_x = lax.ppermute(own, "vx", down_x)
    own_y = lax.ppermute(own, "vy", down_y)
    own_d = lax.ppermute(own, both, down_d)
    def together(rows, cols):
        return jnp.concatenate([fields[:, rows, cols], modulus[None, rows, cols]], axis=0)

    low, full = slice(0, HALO), slice(None)
    beyond_x = lax.ppermute(together(low, full), "vx", down_x)
    corner = lax.ppermute(together(low, low), both, down_d)
    beyond_y = lax.ppermute(together(full, low), "vy", down_y)

    last_x, last_y = tx // HALO - 1, ty // HALO - 1

    def described(spot, from_x, from_y):
        o0, o1, o2, on = (spot[:, k] for k in range(4))
        ok = on > 0
        ok = ok & ((o0 == 0) if from_x else ((o0 > 0) | (i == 0)))
        ok = ok & ((o1 == 0) if from_y else ((o1 > 0) | (j == 0)))
        bx = jnp.full_like(o0, last_x) if from_x else o0 - 1
        by = jnp.full_like(o1, last_y) if from_y else o1 - 1
        kind = jnp.where(bx == last_x, 1, jnp.where(by == last_y, 2, 0))
        return jnp.stack([jnp.where(ok, kind, -1), bx, by, o2], axis=1)

    mine = described(own, False, False)
    everything = jnp.concatenate(
        [
            mine,
            described(own_x, True, False),
            described(own_y, False, True),
            described(own_d, True, True),
        ]
    )
    mats = constants()
    local = (fields, modulus)
    (inner,) = run(0, mine.reshape(-1), [local], mats, tx, ty)
    sources = [local, (beyond_y,), (beyond_x,), (corner,)]
    (strip,) = run(1, everything.reshape(-1), sources, mats, tx, ty, inner)
    from_below = lax.ppermute(strip[HALO:], "vx", up_x)
    owned, side = run(2, everything.reshape(-1), sources[:2], mats, tx, ty, inner, strip)
    side = side.at[:HALO].add(from_below[:, ty:])
    from_left = lax.ppermute(side, "vy", up_y)
    owned = owned.at[:HALO].add(from_below[:, :ty])
    return owned.at[:, :HALO].add(from_left)


def solution(mesh):
    return jax.shard_map(
        shards,
        mesh=mesh,
        in_specs=(
            P(None, "vx", "vy", None),
            P("vx", "vy", None),
            P("vx", "vy", None, None),
            P("vx", "vy"),
        ),
        out_specs=P("vx", "vy", None),
        check_vma=False,
    )
```

profile of v0, /device:TPU:20, one launch (start us, length us, event | category | flops | bytes accessed | tf_op | source)
XLA Modules:
  0.0 186.8 jit_solution(5473135196219520685)
XLA Ops:
  1.5 2.9 %collective-permute-start.2 = (s32[14,4]{0,1:T(4,128)S(1)}, s32[14,4]{0,1:T(4,128)S(1)}, u32[]{:S(2)}, u32[]{:S(2)}) collective-permute-start(s32[14,4]{0,1:T(4,128)S(1)} %pad_add_fusion.1), channel_id=1, source_target_pairs={{5,0},{6,1},{7,2},{9,4},{10,5},{11,6},{13,8},{14,9},{15,10},{17,12... | collective-permute-start | bytes 680 | tf_op jit(solution)/shard_map/ppermute | solution.py:366
  4.4 2.8 %collective-permute-start.1 = (s32[14,4]{0,1:T(4,128)S(1)}, s32[14,4]{0,1:T(4,128)S(1)}, u32[]{:S(2)}, u32[]{:S(2)}) collective-permute-start(s32[14,4]{0,1:T(4,128)S(1)} %pad_add_fusion.1), channel_id=1, source_target_pairs={{1,0},{2,1},{3,2},{5,4},{6,5},{7,6},{9,8},{10,9},{11,10},{13,12},{... | collective-permute-start | bytes 680 | tf_op jit(solution)/shard_map/ppermute | solution.py:365
  7.2 2.4 %collective-permute-start = (s32[14,4]{0,1:T(4,128)S(1)}, s32[14,4]{0,1:T(4,128)S(1)}, u32[]{:S(2)}, u32[]{:S(2)}) collective-permute-start(s32[14,4]{0,1:T(4,128)S(1)} %pad_add_fusion.1), channel_id=1, source_target_pairs={{4,0},{8,4},{12,8},{16,12},{20,16},{24,20},{28,24},{5,1},{9,5},{13... | collective-permute-start | bytes 680 | tf_op jit(solution)/shard_map/ppermute | solution.py:364
  9.6 1.0 slice_bitcast_fusion.1
  10.6 1.2 pad_maximum_fusion.1
  11.8 1.9 %collective-permute-start.3 = (bf16[5,64,16,128]{3,2,1,0:T(8,128)(2,1)}, bf16[5,64,16,128]{3,2,1,0:T(8,128)(2,1)}, u32[]{:S(2)}, u32[]{:S(2)}) collective-permute-start(bf16[5,64,16,128]{3,2,1,0:T(8,128)(2,1)} %pad_maximum_fusion.1), channel_id=1, source_target_pairs={{1,0},{2,1},{3,2},{5,4},{6,5},{7,6},{9,8},{10,9},{11,10},{13,12},{... | collective-permute-start | bytes 3932168 | tf_op jit(solution)/shard_map/ppermute | solution.py:373
  13.8 1.7 slice-done.1
  15.6 2.0 %pad_maximum_fusion = bf16[5,16,160,128]{3,2,1,0:T(8,128)(2,1)} fusion(bf16[1,16,160,128]{3,2,1,0:T(8,128)(2,1)S(1)} %slice_bitcast_fusion, bf16[4,16,160,128]{3,2,1,0:T(8,128)(2,1)S(1)} %slice-done.1), kind=kLoop, calls=%fused_computation | loop fusion | flops 1638400 | bytes 6553600 | tf_op jit(solution)/shard_map/concatenate | solution.py:368
  17.6 3.3 %collective-permute-start.4 = (bf16[5,16,160,128]{3,2,1,0:T(8,128)(2,1)}, bf16[5,16,160,128]{3,2,1,0:T(8,128)(2,1)}, u32[]{:S(2)}, u32[]{:S(2)}) collective-permute-start(bf16[5,16,160,128]{3,2,1,0:T(8,128)(2,1)} %pad_maximum_fusion), channel_id=1, source_target_pairs={{4,0},{8,4},{12,8},{16,12},{20,16},{24,20},{28,24},{5,1},{9,5},{13... | collective-permute-start | bytes 9830408 | tf_op jit(solution)/shard_map/ppermute | solution.py:371
  21.1 1.4 copy-done.1
  22.5 46.9 %interior.1.refs_6_.refs_4_ = f32[64,160,128]{2,1,0:T(8,128)} custom-call(s32[56]{0:T(128)S(1)} %reshape.111.refs_0_, bf16[4,64,160,128]{3,2,1,0:T(8,128)(2,1)} %refs_1_.5, bf16[64,160,128]{2,1,0:T(8,128)(2,1)S(1)} %copy-done, bf16[3,512,512]{2,1,0:T(8,128)(2,1)S(1)} %copy-done.1, bf16[3,128,256]{2,1,0:T(8,128)(2,1)S(1)} %copy-done.4, ...), custom_call_target="tpu_custom_call" | custom-call | flops 20000000000 | bytes 150000000 | tf_op jit(solution)/shard_map/interior/pallas_call | solution.py:325
  69.4 1.0 slice.163
  70.4 1.9 %collective-permute-start.5 = (bf16[5,16,16,128]{3,2,1,0:T(8,128)(2,1)S(1)}, bf16[5,16,16,128]{3,2,1,0:T(8,128)(2,1)S(1)}, u32[]{:S(2)}, u32[]{:S(2)}) collective-permute-start(bf16[5,16,16,128]{3,2,1,0:T(8,128)(2,1)S(1)} %pad_maximum_fusion.2), channel_id=1, source_target_pairs={{5,0},{6,1},{7,2},{9,4},{10,5},{11,6},{13,8},{14,9},{15,10},{17,12... | collective-permute-start | bytes 983048 | tf_op jit(solution)/shard_map/ppermute | solution.py:372
  72.7 27.7 %collective-permute-done.5.refs_5_ = bf16[5,16,16,128]{3,2,1,0:T(8,128)(2,1)S(1)} collective-permute-done((bf16[5,16,16,128]{3,2,1,0:T(8,128)(2,1)S(1)}, bf16[5,16,16,128]{3,2,1,0:T(8,128)(2,1)S(1)}, u32[]{:S(2)}, u32[]{:S(2)}) %collective-permute-start.5) | collective-permute-done | bytes 327712 | tf_op jit(solution)/shard_map/ppermute | solution.py:372
  100.5 1.4 copy-done.2
  101.9 31.2 %beyond_x.1.refs_5_ = f32[32,176,128]{2,1,0:T(8,128)} custom-call(s32[224]{0:T(256)S(1)} %reshape.110.refs_0_, bf16[4,64,160,128]{3,2,1,0:T(8,128)(2,1)} %refs_1_.5, bf16[64,160,128]{2,1,0:T(8,128)(2,1)} %refs_2_.5, bf16[5,64,16,128]{3,2,1,0:T(8,128)(2,1)} %collective-permute-done.3.refs_3_, bf16[5,16,160,128]{3,2,1,0:T(8,128)(2,1)} %collective-permute-done.4.refs_4_, ...), custom_call_target="tpu_custom_call" | custom-call | flops 10000000000 | bytes 150000000 | tf_op jit(solution)/shard_map/beyond_x/pallas_call | solution.py:325
  133.1 1.5 slice.171
  134.5 9.4 %collective-permute-start.6 = (f32[16,176,128]{2,1,0:T(8,128)S(1)}, f32[16,176,128]{2,1,0:T(8,128)S(1)}, u32[]{:S(2)}, u32[]{:S(2)}) collective-permute-start(f32[16,176,128]{2,1,0:T(8,128)S(1)} %slice.171), channel_id=1, source_target_pairs={{0,4},{4,8},{8,12},{12,16},{16,20},{20,24},{24,28},{1,5},{5,9},{9,... | collective-permute-start | bytes 4325384 | tf_op jit(solution)/shard_map/ppermute | solution.py:401
  144.0 6.2 %beyond_y.1 = (f32[64,160,128]{2,1,0:T(8,128)}, f32[64,16,128]{2,1,0:T(8,128)S(1)}) custom-call(s32[224]{0:T(256)S(1)} %reshape.110.refs_0_, bf16[4,64,160,128]{3,2,1,0:T(8,128)(2,1)} %refs_1_.5, bf16[64,160,128]{2,1,0:T(8,128)(2,1)} %refs_2_.5, bf16[5,64,16,128]{3,2,1,0:T(8,128)(2,1)} %collective-permute-done.3.refs_3_, ...), custom_call_target="tpu_custom_call" | custom-call | flops 10000000000 | bytes 150000000 | tf_op jit(solution)/shard_map/beyond_y/pallas_call | solution.py:325
  150.2 24.1 %collective-permute-done.6 = f32[16,176,128]{2,1,0:T(8,128)S(1)} collective-permute-done((f32[16,176,128]{2,1,0:T(8,128)S(1)}, f32[16,176,128]{2,1,0:T(8,128)S(1)}, u32[]{:S(2)}, u32[]{:S(2)}) %collective-permute-start.6) | collective-permute-done | bytes 1441824 | tf_op jit(solution)/shard_map/ppermute | solution.py:401
  174.4 3.6 %collective-permute-start.7 = (f32[64,16,128]{2,1,0:T(8,128)S(1)}, f32[64,16,128]{2,1,0:T(8,128)S(1)}, u32[]{:S(2)}, u32[]{:S(2)}) collective-permute-start(f32[64,16,128]{2,1,0:T(8,128)S(1)} %fusion.2), channel_id=1, source_target_pairs={{0,1},{1,2},{2,3},{4,5},{5,6},{6,7},{8,9},{9,10},{10,11},{12,13},{... | collective-permute-start | bytes 1572872 | tf_op jit(solution)/shard_map/ppermute | solution.py:404
  178.0 2.5 %fusion = f32[64,160,128]{2,1,0:T(8,128)} fusion(f32[64,160,128]{2,1,0:T(8,128)} %get-tuple-element.43, f32[16,176,128]{2,1,0:T(8,128)S(1)} %collective-permute-done.6), kind=kLoop, calls=%fused_computation.2 | loop fusion | flops 327680 | bytes 3932160 | tf_op jit(solution)/shard_map/scatter-add | solution.py:405
  180.5 4.4 %collective-permute-done.7 = f32[64,16,128]{2,1,0:T(8,128)S(1)} collective-permute-done((f32[64,16,128]{2,1,0:T(8,128)S(1)}, f32[64,16,128]{2,1,0:T(8,128)S(1)}, u32[]{:S(2)}, u32[]{:S(2)}) %collective-permute-start.7) | collective-permute-done | bytes 524320 | tf_op jit(solution)/shard_map/ppermute | solution.py:404
  184.9 1.9 %fusion.1 = f32[64,160,128]{2,1,0:T(8,128)} fusion(f32[64,160,128]{2,1,0:T(8,128)} %fusion, f32[64,16,128]{2,1,0:T(8,128)S(1)} %collective-permute-done.7), kind=kLoop, calls=%fused_computation.6 | loop fusion | flops 131072 | bytes 1572864 | tf_op jit(solution)/shard_map/scatter-add | solution.py:406
  (37 shorter events, 1.4 us)
Async XLA Ops:
  0.0 10.6 %slice-start = ((bf16[4,64,160,128]{3,2,1,0:T(8,128)(2,1)}), bf16[4,64,16,128]{3,2,1,0:T(8,128)(2,1)S(1)}, s32[]{:S(2)}) async-start(bf16[4,64,160,128]{3,2,1,0:T(8,128)(2,1)} %refs_1_.5), calls=%async_computation | async-start | bytes 2097152 | tf_op jit(solution)/shard_map/slice | solution.py:368
  1.5 12.3 %copy-start = (bf16[64,160,128]{2,1,0:T(8,128)(2,1)S(1)}, bf16[64,160,128]{2,1,0:T(8,128)(2,1)}, u32[]{:S(2)}) copy-start(bf16[64,160,128]{2,1,0:T(8,128)(2,1)} %refs_2_.5) | copy-start | bytes 7864324
  1.5 71.0 %collective-permute-start.2 = (s32[14,4]{0,1:T(4,128)S(1)}, s32[14,4]{0,1:T(4,128)S(1)}, u32[]{:S(2)}, u32[]{:S(2)}) collective-permute-start(s32[14,4]{0,1:T(4,128)S(1)} %pad_add_fusion.1), channel_id=1, source_target_pairs={{5,0},{6,1},{7,2},{9,4},{10,5},{11,6},{13,8},{14,9},{15,10},{17,12... | collective-permute-start | bytes 680 | tf_op jit(solution)/shard_map/ppermute | solution.py:366
  4.4 66.0 %collective-permute-start.1 = (s32[14,4]{0,1:T(4,128)S(1)}, s32[14,4]{0,1:T(4,128)S(1)}, u32[]{:S(2)}, u32[]{:S(2)}) collective-permute-start(s32[14,4]{0,1:T(4,128)S(1)} %pad_add_fusion.1), channel_id=1, source_target_pairs={{1,0},{2,1},{3,2},{5,4},{6,5},{7,6},{9,8},{10,9},{11,10},{13,12},{... | collective-permute-start | bytes 680 | tf_op jit(solution)/shard_map/ppermute | solution.py:365
  7.2 65.2 %collective-permute-start = (s32[14,4]{0,1:T(4,128)S(1)}, s32[14,4]{0,1:T(4,128)S(1)}, u32[]{:S(2)}, u32[]{:S(2)}) collective-permute-start(s32[14,4]{0,1:T(4,128)S(1)} %pad_add_fusion.1), channel_id=1, source_target_pairs={{4,0},{8,4},{12,8},{16,12},{20,16},{24,20},{28,24},{5,1},{9,5},{13... | collective-permute-start | bytes 680 | tf_op jit(solution)/shard_map/ppermute | solution.py:364
  11.8 88.6 %collective-permute-start.3 = (bf16[5,64,16,128]{3,2,1,0:T(8,128)(2,1)}, bf16[5,64,16,128]{3,2,1,0:T(8,128)(2,1)}, u32[]{:S(2)}, u32[]{:S(2)}) collective-permute-start(bf16[5,64,16,128]{3,2,1,0:T(8,128)(2,1)} %pad_maximum_fusion.1), channel_id=1, source_target_pairs={{1,0},{2,1},{3,2},{5,4},{6,5},{7,6},{9,8},{10,9},{11,10},{13,12},{... | collective-permute-start | bytes 3932168 | tf_op jit(solution)/shard_map/ppermute | solution.py:373
  13.8 1.7 slice-start.1
  15.6 5.5 %copy-start.3 = (bf16[3,512,128]{2,1,0:T(8,128)(2,1)S(1)}, bf16[3,512,128]{2,1,0:T(8,128)(2,1)}, u32[]{:S(2)}) copy-start(bf16[3,512,128]{2,1,0:T(8,128)(2,1)} %constant.111.clone.refs_5_.refs_9_.refs_8_) | copy-start | bytes 1179652
  15.6 5.5 %copy-start.4 = (bf16[3,128,256]{2,1,0:T(8,128)(2,1)S(1)}, bf16[3,128,256]{2,1,0:T(8,128)(2,1)}, u32[]{:S(2)}) copy-start(bf16[3,128,256]{2,1,0:T(8,128)(2,1)} %constant.110.clone.refs_4_.refs_8_.refs_7_) | copy-start | bytes 589828
  15.6 5.5 %copy-start.5 = (bf16[256,128]{1,0:T(8,128)(2,1)S(1)}, bf16[256,128]{1,0:T(8,128)(2,1)}, u32[]{:S(2)}) copy-start(bf16[256,128]{1,0:T(8,128)(2,1)} %constant.112.clone.refs_6_.refs_10_.refs_9_) | copy-start | bytes 196612
  17.6 82.9 %collective-permute-start.4 = (bf16[5,16,160,128]{3,2,1,0:T(8,128)(2,1)}, bf16[5,16,160,128]{3,2,1,0:T(8,128)(2,1)}, u32[]{:S(2)}, u32[]{:S(2)}) collective-permute-start(bf16[5,16,160,128]{3,2,1,0:T(8,128)(2,1)} %pad_maximum_fusion), channel_id=1, source_target_pairs={{4,0},{8,4},{12,8},{16,12},{20,16},{24,20},{28,24},{5,1},{9,5},{13... | collective-permute-start | bytes 9830408 | tf_op jit(solution)/shard_map/ppermute | solution.py:371
  21.1 1.4 copy-start.1
  70.4 30.0 %collective-permute-start.5 = (bf16[5,16,16,128]{3,2,1,0:T(8,128)(2,1)S(1)}, bf16[5,16,16,128]{3,2,1,0:T(8,128)(2,1)S(1)}, u32[]{:S(2)}, u32[]{:S(2)}) collective-permute-start(bf16[5,16,16,128]{3,2,1,0:T(8,128)(2,1)S(1)} %pad_maximum_fusion.2), channel_id=1, source_target_pairs={{5,0},{6,1},{7,2},{9,4},{10,5},{11,6},{13,8},{14,9},{15,10},{17,12... | collective-permute-start | bytes 983048 | tf_op jit(solution)/shard_map/ppermute | solution.py:372
  100.5 1.4 copy-start.2
  134.5 39.8 %collective-permute-start.6 = (f32[16,176,128]{2,1,0:T(8,128)S(1)}, f32[16,176,128]{2,1,0:T(8,128)S(1)}, u32[]{:S(2)}, u32[]{:S(2)}) collective-permute-start(f32[16,176,128]{2,1,0:T(8,128)S(1)} %slice.171), channel_id=1, source_target_pairs={{0,4},{4,8},{8,12},{12,16},{16,20},{20,24},{24,28},{1,5},{5,9},{9,... | collective-permute-start | bytes 4325384 | tf_op jit(solution)/shard_map/ppermute | solution.py:401
  174.4 10.5 %collective-permute-start.7 = (f32[64,16,128]{2,1,0:T(8,128)S(1)}, f32[64,16,128]{2,1,0:T(8,128)S(1)}, u32[]{:S(2)}, u32[]{:S(2)}) collective-permute-start(f32[64,16,128]{2,1,0:T(8,128)S(1)} %fusion.2), channel_id=1, source_target_pairs={{0,1},{1,2},{2,3},{4,5},{5,6},{6,7},{8,9},{9,10},{10,11},{12,13},{... | collective-permute-start | bytes 1572872 | tf_op jit(solution)/shard_map/ppermute | solution.py:404
where the time goes:
time: 190 us; the launch traced here: 187 us
  Pallas kernels  84.3 us (44%)
  waiting for transfers between devices  56.2 us (30%)
  starting transfers between devices  28.3 us (15%)
  local copies, waits for them, and re-layouts  9.1 us (5%)
  other arithmetic  7.85 us (4%)
    pallas_call x3, Pallas kernels, run(): pl.pallas_call(functools.partial(work, group, slots, group, tx, ty, len(s...  84.3 us
    ppermute x1, waiting for transfers between devices, shards(): corner = lax.ppermute(together(low, low), both, down_d)  27.7 us
    ppermute x1, waiting for transfers between devices, shards(): from_below = lax.ppermute(strip[HALO:], 'vx', up_x)  24.1 us
    ppermute x1, starting transfers between devices, shards(): from_below = lax.ppermute(strip[HALO:], 'vx', up_x)  9.45 us
    ppermute x1, waiting for transfers between devices, shards(): from_left = lax.ppermute(side, 'vy', up_y)  4.38 us
  transfers between devices with their start and end apart: 8, of which 3 were waited for; matrix products, arithmetic and copies ran while one was open for 4% of the time, Pallas kernels for 28%

commit v1 on v0

--- a/solution.py
+++ b/solution.py
@@ -14,8 +14,8 @@
 OMEGA = 0.07
 LANES = 128
 NZ = 64
-PLANES = 8
-A_PLANES = 8
+PLANES = 16
+A_PLANES = 16
 FIRST = 8
 
 
@@ -362,8 +362,7 @@
     live = (jnp.arange(home, dtype=jnp.int32) < home_count[0, 0]).astype(jnp.int32)
     own = jnp.concatenate([spots, live[:, None]], axis=1)
     own_x = lax.ppermute(own, "vx", down_x)
-    own_y = lax.ppermute(own, "vy", down_y)
-    own_d = lax.ppermute(own, both, down_d)
+    own_y, own_d = jnp.split(lax.ppermute(jnp.concatenate([own, own_x]), "vy", down_y), 2)
     def together(rows, cols):
         return jnp.concatenate([fields[:, rows, cols], modulus[None, rows, cols]], axis=0)
 
@@ -395,7 +394,7 @@
     )
     mats = constants()
     local = (fields, modulus)
-    (inner,) = run(0, mine.reshape(-1), [local], mats, tx, ty)
+    (inner,) = run(0, everything.reshape(-1), [local], mats, tx, ty)
     sources = [local, (beyond_y,), (beyond_x,), (corner,)]
     (strip,) = run(1, everything.reshape(-1), sources, mats, tx, ty, inner)
     from_below = lax.ppermute(strip[HALO:], "vx", up_x)

time: 190 us -> 170 us (0.89)
  the two profiles are of different devices: /device:TPU:20 before, /device:TPU:14 now
where the time goes in v1:
time: 170 us; the launch traced here: 171 us
  waiting for transfers between devices  70.7 us (42%)
  Pallas kernels  54.4 us (32%)
  starting transfers between devices  26.9 us (16%)
  local copies, waits for them, and re-layouts  9.82 us (6%)
  other arithmetic  8.74 us (5%)
    pallas_call x3, Pallas kernels, run(): pl.pallas_call(functools.partial(work, group, slots, group, tx, ty, len(s...  54.4 us
    ppermute x1, waiting for transfers between devices, shards(): corner = lax.ppermute(together(low, low), both, down_d)  28.5 us
    ppermute x1, waiting for transfers between devices, shards(): from_below = lax.ppermute(strip[HALO:], 'vx', up_x)  24.3 us
    ppermute x1, waiting for transfers between devices, shards(): lax.ppermute(jnp.concatenate([own, own_x]), 'vy', down_y)  13.4 us
    ppermute x1, starting transfers between devices, shards(): from_below = lax.ppermute(strip[HALO:], 'vx', up_x)  11.6 us
    ppermute x1, waiting for transfers between devices, shards(): from_left = lax.ppermute(side, 'vy', up_y)  4.5 us
    concatenate x3, other arithmetic, together(): jnp.concatenate([fields[:, rows, cols], modulus[None, rows, cols]], axis=0)  3.97 us
    ppermute x1, starting transfers between devices, shards(): from_left = lax.ppermute(side, 'vy', up_y)  3.43 us
  transfers between devices with their start and end apart: 7, of which 4 were waited for; matrix products, arithmetic and copies ran while one was open for 6% of the time, Pallas kernels for 17%

profile of v1, /device:TPU:14, one launch (start us, length us, event | category | flops | bytes accessed | tf_op | source)
XLA Modules:
  0.0 171.5 jit_solution(14988645694780830056)
XLA Ops:
  1.4 2.4 %collective-permute-start = (s32[14,4]{0,1:T(4,128)S(1)}, s32[14,4]{0,1:T(4,128)S(1)}, u32[]{:S(2)}, u32[]{:S(2)}) collective-permute-start(s32[14,4]{0,1:T(4,128)S(1)} %pad_add_fusion), channel_id=1, source_target_pairs={{4,0},{8,4},{12,8},{16,12},{20,16},{24,20},{28,24},{5,1},{9,5},{13... | collective-permute-start | bytes 680 | tf_op jit(solution)/shard_map/ppermute | solution.py:364
  3.8 1.1 slice_bitcast_fusion
  5.0 1.7 %slice-done = bf16[4,16,160,128]{3,2,1,0:T(8,128)(2,1)S(1)} async-done(((bf16[4,64,160,128]{3,2,1,0:T(8,128)(2,1)}), bf16[4,16,160,128]{3,2,1,0:T(8,128)(2,1)S(1)}, s32[]{:S(2)}) %slice-start) | async-done | bytes 2621464 | tf_op jit(solution)/shard_map/slice | solution.py:367
  6.7 2.0 %pad_maximum_fusion = bf16[5,16,160,128]{3,2,1,0:T(8,128)(2,1)} fusion(bf16[1,16,160,128]{3,2,1,0:T(8,128)(2,1)S(1)} %slice_bitcast_fusion, bf16[4,16,160,128]{3,2,1,0:T(8,128)(2,1)S(1)} %slice-done), kind=kLoop, calls=%fused_computation | loop fusion | flops 1638400 | bytes 6553600 | tf_op jit(solution)/shard_map/concatenate | solution.py:367
  8.7 3.4 %collective-permute-start.3 = (bf16[5,16,160,128]{3,2,1,0:T(8,128)(2,1)}, bf16[5,16,160,128]{3,2,1,0:T(8,128)(2,1)}, u32[]{:S(2)}, u32[]{:S(2)}) collective-permute-start(bf16[5,16,160,128]{3,2,1,0:T(8,128)(2,1)} %pad_maximum_fusion), channel_id=1, source_target_pairs={{4,0},{8,4},{12,8},{16,12},{20,16},{24,20},{28,24},{5,1},{9,5},{13... | collective-permute-start | bytes 9830408 | tf_op jit(solution)/shard_map/ppermute | solution.py:370
  12.1 1.0 slice.171
  13.9 2.0 %collective-permute-start.4 = (bf16[5,16,16,128]{3,2,1,0:T(8,128)(2,1)}, bf16[5,16,16,128]{3,2,1,0:T(8,128)(2,1)S(1)}, u32[]{:S(2)}, u32[]{:S(2)}) collective-permute-start(bf16[5,16,16,128]{3,2,1,0:T(8,128)(2,1)} %pad_maximum_fusion.2), channel_id=1, source_target_pairs={{5,0},{6,1},{7,2},{9,4},{10,5},{11,6},{13,8},{14,9},{15,10},{17,12... | collective-permute-start | bytes 983048 | tf_op jit(solution)/shard_map/ppermute | solution.py:371
  16.0 1.2 pad_maximum_fusion.1
  17.2 2.1 %collective-permute-start.2 = (bf16[5,64,16,128]{3,2,1,0:T(8,128)(2,1)}, bf16[5,64,16,128]{3,2,1,0:T(8,128)(2,1)}, u32[]{:S(2)}, u32[]{:S(2)}) collective-permute-start(bf16[5,64,16,128]{3,2,1,0:T(8,128)(2,1)} %pad_maximum_fusion.1), channel_id=1, source_target_pairs={{1,0},{2,1},{3,2},{5,4},{6,5},{7,6},{9,8},{10,9},{11,10},{13,12},{... | collective-permute-start | bytes 3932168 | tf_op jit(solution)/shard_map/ppermute | solution.py:372
  19.4 1.9 %collective-permute-start.1 = (s32[28,4]{0,1:T(4,128)S(1)}, s32[28,4]{0,1:T(4,128)S(1)}, u32[]{:S(2)}, u32[]{:S(2)}) collective-permute-start(s32[28,4]{0,1:T(4,128)S(1)} %pad_add_fusion.1), channel_id=1, source_target_pairs={{1,0},{2,1},{3,2},{5,4},{6,5},{7,6},{9,8},{10,9},{11,10},{13,12},{... | collective-permute-start | bytes 1352 | tf_op jit(solution)/shard_map/ppermute | solution.py:365
  21.4 13.4 %collective-permute-done.1 = s32[28,4]{0,1:T(4,128)S(1)} collective-permute-done((s32[28,4]{0,1:T(4,128)S(1)}, s32[28,4]{0,1:T(4,128)S(1)}, u32[]{:S(2)}, u32[]{:S(2)}) %collective-permute-start.1) | collective-permute-done | bytes 480 | tf_op jit(solution)/shard_map/ppermute | solution.py:365
  35.6 0.8 reshape.108.refs_0_
  36.5 1.4 copy-done.1
  38.7 22.5 %interior.1.refs_6_.refs_4_ = f32[64,160,128]{2,1,0:T(8,128)} custom-call(s32[224]{0:T(256)S(1)} %reshape.108.refs_0_, bf16[4,64,160,128]{3,2,1,0:T(8,128)(2,1)} %refs_1_.5, bf16[64,160,128]{2,1,0:T(8,128)(2,1)S(1)} %copy-done, bf16[3,512,512]{2,1,0:T(8,128)(2,1)S(1)} %copy-done.1, bf16[3,128,256]{2,1,0:T(8,128)(2,1)S(1)} %copy-done.3, ...), custom_call_target="tpu_custom_call" | custom-call | flops 20000000000 | bytes 150000000 | tf_op jit(solution)/shard_map/interior/pallas_call | solution.py:325
  61.2 28.5 %collective-permute-done.4.refs_5_ = bf16[5,16,16,128]{3,2,1,0:T(8,128)(2,1)S(1)} collective-permute-done((bf16[5,16,16,128]{3,2,1,0:T(8,128)(2,1)}, bf16[5,16,16,128]{3,2,1,0:T(8,128)(2,1)S(1)}, u32[]{:S(2)}, u32[]{:S(2)}) %collective-permute-start.4) | collective-permute-done | bytes 327712 | tf_op jit(solution)/shard_map/ppermute | solution.py:371
  89.7 25.7 %beyond_x.1.refs_5_ = f32[32,176,128]{2,1,0:T(8,128)} custom-call(s32[224]{0:T(256)S(1)} %reshape.108.refs_0_, bf16[4,64,160,128]{3,2,1,0:T(8,128)(2,1)} %refs_1_.5, bf16[64,160,128]{2,1,0:T(8,128)(2,1)} %refs_2_.5, bf16[5,64,16,128]{3,2,1,0:T(8,128)(2,1)} %collective-permute-done.2.refs_3_, bf16[5,16,160,128]{3,2,1,0:T(8,128)(2,1)} %collective-permute-done.3.refs_4_, ...), custom_call_target="tpu_custom_call" | custom-call | flops 10000000000 | bytes 150000000 | tf_op jit(solution)/shard_map/beyond_x/pallas_call | solution.py:325
  115.4 1.5 slice.179
  116.9 11.6 %collective-permute-start.5 = (f32[16,176,128]{2,1,0:T(8,128)S(1)}, f32[16,176,128]{2,1,0:T(8,128)S(1)}, u32[]{:S(2)}, u32[]{:S(2)}) collective-permute-start(f32[16,176,128]{2,1,0:T(8,128)S(1)} %slice.179), channel_id=1, source_target_pairs={{0,4},{4,8},{8,12},{12,16},{16,20},{20,24},{24,28},{1,5},{5,9},{9,... | collective-permute-start | bytes 4325384 | tf_op jit(solution)/shard_map/ppermute | solution.py:400
  128.5 6.2 %beyond_y.1 = (f32[64,160,128]{2,1,0:T(8,128)}, f32[64,16,128]{2,1,0:T(8,128)S(1)}) custom-call(s32[224]{0:T(256)S(1)} %reshape.108.refs_0_, bf16[4,64,160,128]{3,2,1,0:T(8,128)(2,1)} %refs_1_.5, bf16[64,160,128]{2,1,0:T(8,128)(2,1)} %refs_2_.5, bf16[5,64,16,128]{3,2,1,0:T(8,128)(2,1)} %collective-permute-done.2.refs_3_, ...), custom_call_target="tpu_custom_call" | custom-call | flops 10000000000 | bytes 150000000 | tf_op jit(solution)/shard_map/beyond_y/pallas_call | solution.py:325
  134.7 24.3 %collective-permute-done.5 = f32[16,176,128]{2,1,0:T(8,128)S(1)} collective-permute-done((f32[16,176,128]{2,1,0:T(8,128)S(1)}, f32[16,176,128]{2,1,0:T(8,128)S(1)}, u32[]{:S(2)}, u32[]{:S(2)}) %collective-permute-start.5) | collective-permute-done | bytes 1441824 | tf_op jit(solution)/shard_map/ppermute | solution.py:400
  159.0 3.4 %collective-permute-start.6 = (f32[64,16,128]{2,1,0:T(8,128)S(1)}, f32[64,16,128]{2,1,0:T(8,128)S(1)}, u32[]{:S(2)}, u32[]{:S(2)}) collective-permute-start(f32[64,16,128]{2,1,0:T(8,128)S(1)} %fusion.2), channel_id=1, source_target_pairs={{0,1},{1,2},{2,3},{4,5},{5,6},{6,7},{8,9},{9,10},{10,11},{12,13},{... | collective-permute-start | bytes 1572872 | tf_op jit(solution)/shard_map/ppermute | solution.py:403
  162.5 2.6 %fusion = f32[64,160,128]{2,1,0:T(8,128)} fusion(f32[64,160,128]{2,1,0:T(8,128)} %get-tuple-element.43, f32[16,176,128]{2,1,0:T(8,128)S(1)} %collective-permute-done.5), kind=kLoop, calls=%fused_computation.2 | loop fusion | flops 327680 | bytes 3932160 | tf_op jit(solution)/shard_map/scatter-add | solution.py:404
  165.0 4.5 %collective-permute-done.6 = f32[64,16,128]{2,1,0:T(8,128)S(1)} collective-permute-done((f32[64,16,128]{2,1,0:T(8,128)S(1)}, f32[64,16,128]{2,1,0:T(8,128)S(1)}, u32[]{:S(2)}, u32[]{:S(2)}) %collective-permute-start.6) | collective-permute-done | bytes 524320 | tf_op jit(solution)/shard_map/ppermute | solution.py:403
  169.5 1.9 %fusion.1 = f32[64,160,128]{2,1,0:T(8,128)} fusion(f32[64,160,128]{2,1,0:T(8,128)} %fusion, f32[64,16,128]{2,1,0:T(8,128)S(1)} %collective-permute-done.6), kind=kLoop, calls=%fused_computation.6 | loop fusion | flops 131072 | bytes 1572864 | tf_op jit(solution)/shard_map/scatter-add | solution.py:405
  (30 shorter events, 3.3 us)
Async XLA Ops:
  1.4 18.0 %collective-permute-start = (s32[14,4]{0,1:T(4,128)S(1)}, s32[14,4]{0,1:T(4,128)S(1)}, u32[]{:S(2)}, u32[]{:S(2)}) collective-permute-start(s32[14,4]{0,1:T(4,128)S(1)} %pad_add_fusion), channel_id=1, source_target_pairs={{4,0},{8,4},{12,8},{16,12},{20,16},{24,20},{28,24},{5,1},{9,5},{13... | collective-permute-start | bytes 680 | tf_op jit(solution)/shard_map/ppermute | solution.py:364
  4.9 1.7 %slice-start = ((bf16[4,64,160,128]{3,2,1,0:T(8,128)(2,1)}), bf16[4,16,160,128]{3,2,1,0:T(8,128)(2,1)S(1)}, s32[]{:S(2)}) async-start(bf16[4,64,160,128]{3,2,1,0:T(8,128)(2,1)} %refs_1_.5), calls=%async_computation | async-start | bytes 5242880 | tf_op jit(solution)/shard_map/slice | solution.py:367
  6.7 5.4 %copy-start = (bf16[64,160,128]{2,1,0:T(8,128)(2,1)S(1)}, bf16[64,160,128]{2,1,0:T(8,128)(2,1)}, u32[]{:S(2)}) copy-start(bf16[64,160,128]{2,1,0:T(8,128)(2,1)} %refs_2_.5) | copy-start | bytes 7864324
  8.7 7.3 %slice-start.1 = ((bf16[4,64,160,128]{3,2,1,0:T(8,128)(2,1)}), bf16[4,64,16,128]{3,2,1,0:T(8,128)(2,1)S(1)}, s32[]{:S(2)}) async-start(bf16[4,64,160,128]{3,2,1,0:T(8,128)(2,1)} %refs_1_.5), calls=%async_computation.1 | async-start | bytes 2097152 | tf_op jit(solution)/shard_map/slice | solution.py:367
  8.7 81.1 %collective-permute-start.3 = (bf16[5,16,160,128]{3,2,1,0:T(8,128)(2,1)}, bf16[5,16,160,128]{3,2,1,0:T(8,128)(2,1)}, u32[]{:S(2)}, u32[]{:S(2)}) collective-permute-start(bf16[5,16,160,128]{3,2,1,0:T(8,128)(2,1)} %pad_maximum_fusion), channel_id=1, source_target_pairs={{4,0},{8,4},{12,8},{16,12},{20,16},{24,20},{28,24},{5,1},{9,5},{13... | collective-permute-start | bytes 9830408 | tf_op jit(solution)/shard_map/ppermute | solution.py:370
  13.9 22.6 %copy-start.2 = (bf16[3,512,128]{2,1,0:T(8,128)(2,1)S(1)}, bf16[3,512,128]{2,1,0:T(8,128)(2,1)}, u32[]{:S(2)}) copy-start(bf16[3,512,128]{2,1,0:T(8,128)(2,1)} %constant.111.clone.refs_5_.refs_9_.refs_8_) | copy-start | bytes 1179652
  13.9 22.6 %copy-start.3 = (bf16[3,128,256]{2,1,0:T(8,128)(2,1)S(1)}, bf16[3,128,256]{2,1,0:T(8,128)(2,1)}, u32[]{:S(2)}) copy-start(bf16[3,128,256]{2,1,0:T(8,128)(2,1)} %constant.110.clone.refs_4_.refs_8_.refs_7_) | copy-start | bytes 589828
  13.9 75.9 %collective-permute-start.4 = (bf16[5,16,16,128]{3,2,1,0:T(8,128)(2,1)}, bf16[5,16,16,128]{3,2,1,0:T(8,128)(2,1)S(1)}, u32[]{:S(2)}, u32[]{:S(2)}) collective-permute-start(bf16[5,16,16,128]{3,2,1,0:T(8,128)(2,1)} %pad_maximum_fusion.2), channel_id=1, source_target_pairs={{5,0},{6,1},{7,2},{9,4},{10,5},{11,6},{13,8},{14,9},{15,10},{17,12... | collective-permute-start | bytes 983048 | tf_op jit(solution)/shard_map/ppermute | solution.py:371
  17.2 72.6 %collective-permute-start.2 = (bf16[5,64,16,128]{3,2,1,0:T(8,128)(2,1)}, bf16[5,64,16,128]{3,2,1,0:T(8,128)(2,1)}, u32[]{:S(2)}, u32[]{:S(2)}) collective-permute-start(bf16[5,64,16,128]{3,2,1,0:T(8,128)(2,1)} %pad_maximum_fusion.1), channel_id=1, source_target_pairs={{1,0},{2,1},{3,2},{5,4},{6,5},{7,6},{9,8},{10,9},{11,10},{13,12},{... | collective-permute-start | bytes 3932168 | tf_op jit(solution)/shard_map/ppermute | solution.py:372
  19.4 15.3 %collective-permute-start.1 = (s32[28,4]{0,1:T(4,128)S(1)}, s32[28,4]{0,1:T(4,128)S(1)}, u32[]{:S(2)}, u32[]{:S(2)}) collective-permute-start(s32[28,4]{0,1:T(4,128)S(1)} %pad_add_fusion.1), channel_id=1, source_target_pairs={{1,0},{2,1},{3,2},{5,4},{6,5},{7,6},{9,8},{10,9},{11,10},{13,12},{... | collective-permute-start | bytes 1352 | tf_op jit(solution)/shard_map/ppermute | solution.py:365
  36.5 1.4 copy-start.1
  37.9 0.8 copy-start.4
  116.9 42.1 %collective-permute-start.5 = (f32[16,176,128]{2,1,0:T(8,128)S(1)}, f32[16,176,128]{2,1,0:T(8,128)S(1)}, u32[]{:S(2)}, u32[]{:S(2)}) collective-permute-start(f32[16,176,128]{2,1,0:T(8,128)S(1)} %slice.179), channel_id=1, source_target_pairs={{0,4},{4,8},{8,12},{12,16},{16,20},{20,24},{24,28},{1,5},{5,9},{9,... | collective-permute-start | bytes 4325384 | tf_op jit(solution)/shard_map/ppermute | solution.py:400
  159.0 10.5 %collective-permute-start.6 = (f32[64,16,128]{2,1,0:T(8,128)S(1)}, f32[64,16,128]{2,1,0:T(8,128)S(1)}, u32[]{:S(2)}, u32[]{:S(2)}) collective-permute-start(f32[64,16,128]{2,1,0:T(8,128)S(1)} %fusion.2), channel_id=1, source_target_pairs={{0,1},{1,2},{2,3},{4,5},{5,6},{6,7},{8,9},{9,10},{10,11},{12,13},{... | collective-permute-start | bytes 1572872 | tf_op jit(solution)/shard_map/ppermute | solution.py:403
